TPU v7x, 256 devices: a whole 4x4x8 slice. The times are simulated.
256 devices in a mesh: replica: 32 (over x, z), shard: 8 (over y, core).
Axes of the slice: x: 4, y: 4, z: 8, core: 2. Of those that a mesh axis runs over, the one named last changes fastest.
Arguments:
- grads: bfloat16 [32, 8192, 2048], P('replica', 'shard'), may hold values from -64 to 64
- errors: bfloat16 [32, 8192, 2048], P('replica', 'shard'), may hold values from -4 to 4
- q_prev: bfloat16 [32, 2048], P(None, 'shard'), may hold values from -6 to 6
- momentum: float32 [8192, 2048], P('shard', 'replica'), may hold values from -1.2 to 1.2
Outputs:
- new_errors: bfloat16 [32, 8192, 2048], P('replica', 'shard')
- new_momentum: float32 [8192, 2048], P('shard', 'replica')
- q_next: float32 [32, 2048], P(None, 'shard')
All inputs are finite; a program needn't handle non-finite values.
Results may differ from a plain program's by a relative error of at most 0.012.
Values may be sent and summed in bfloat16 or wider, within the bound.
A program may use at most 64 MiB of HBM per device.

v0:
```python
import jax
import jax.numpy as jnp
from jax import lax
from jax.sharding import PartitionSpec as P


def shards(grads, errors, q_prev, momentum):
    highest = lax.Precision.HIGHEST
    merged = grads[0].astype(jnp.float32) + errors[0].astype(jnp.float32)
    col_count = merged.shape[1]
    product = lax.dot_general(
        merged,
        lax.all_gather(q_prev, "shard", axis=1, tiled=True).astype(jnp.float32),
        (((1,), (1,)), ((), ())),
        precision=highest,
    )
    factor = lax.psum(product.astype(jnp.bfloat16), "replica").astype(jnp.float32)
    every_row = lax.all_gather(factor.astype(jnp.bfloat16), "shard", axis=0, tiled=True).astype(
        factor.dtype
    )
    gram_matrix = jnp.dot(every_row.T, every_row, precision=highest)
    lower_factor = jnp.linalg.cholesky(gram_matrix)
    ortho = jax.scipy.linalg.solve_triangular(lower_factor, factor.T, lower=True).T
    right_term = jnp.dot(ortho.T, merged, precision=highest)
    replicas = lax.axis_size("replica")
    block_width = col_count // lax.axis_size("shard")
    right_full = lax.psum(right_term, ("replica", "shard")) / replicas
    q_next = lax.dynamic_slice_in_dim(
        right_full, lax.axis_index("shard") * block_width, block_width, 1
    )
    approx = jnp.dot(ortho, right_full, precision=highest)
    new_errors = (merged - approx).astype(jnp.bfloat16)[None]
    momentum_width = momentum.shape[1]
    approx_block = lax.dynamic_slice_in_dim(
        approx, lax.axis_index("replica") * momentum_width, momentum_width, 1
    )
    new_momentum = 0.9 * momentum + approx_block
    return (new_errors, new_momentum, q_next)


def solution(mesh):
    return jax.shard_map(
        shards,
        mesh=mesh,
        in_specs=(
            P("replica", "shard", None),
            P("replica", "shard", None),
            P(None, "shard"),
            P("shard", "replica"),
        ),
        out_specs=(P("replica", "shard", None), P("shard", "replica"), P(None, "shard")),
        check_vma=False,
    )
```

profile of v0, /device:TPU:2, one launch (start us, length us, event | category | flops | bytes accessed | tf_op | source)
XLA Modules:
  0.0 478.8 jit_solution(6031099820396762904)
XLA Ops:
  7.2 0.0 all-reduce.3.cloned.1.call-start
  7.2 13.5 %all_gather.6 = bf16[32,2048]{1,0:T(8,128)(2,1)S(1)} all-gather(bf16[32,256]{1,0:T(8,128)(2,1)} %param.6), channel_id=1, replica_groups=mesh['replica'=32,'shard'=8] {'shard'}, dimensions={1}, use_global_device_ids=true | all-gather | bytes 147456 | tf_op jit(solution)/shard_map/all_gather | solution.py:13
  20.7 0.0 copy-start.2
  20.7 9.1 %fusion.6 = bf16[1024,32]{0,1:T(8,128)(2,1)} fusion(bf16[32,2048]{1,0:T(8,128)(2,1)S(1)} %all_gather.6, bf16[1,1024,2048]{2,1,0:T(8,128)(2,1)} %param.5, bf16[1,1024,2048]{2,1,0:T(8,128)(2,1)} %param.4), kind=kOutput, calls=%fused_computation.8 | convolution fusion | flops 811630592 | bytes 8585216 | tf_op jit(solution)/shard_map/dot_general | solution.py:11
  29.8 0.0 all-reduce.3.cloned.1.call-update
  29.8 0.0 all-reduce.5.cloned.1.call-start
  29.8 141.3 %all-reduce.3.cloned.1.call-done = bf16[1024,32]{0,1:T(8,128)(2,1)} async-done(((bf16[1024,32]{0,1:T(8,128)(2,1)}), bf16[1024,32]{0,1:T(8,128)(2,1)}) %all-reduce.3.cloned.1.call-update) | async-done | bytes 65552 | tf_op jit(solution)/shard_map/psum | solution.py:17
  171.2 13.8 %all_gather.7 = bf16[8192,32]{0,1:T(8,128)(2,1)S(1)} all-gather(bf16[1024,32]{0,1:T(8,128)(2,1)} %all-reduce.3.cloned.1.call-done), channel_id=1, replica_groups=mesh['replica'=32,'shard'=8] {'shard'}, dimensions={0}, use_global_device_ids=true | all-gather | bytes 589824 | tf_op jit(solution)/shard_map/all_gather | solution.py:18
  185.0 0.3 fusion.14
  185.3 0.1 copy.7
  185.4 2.9 cholesky.16
  188.3 0.6 compare_reduce_fusion
  189.0 0.7 fusion.9
  189.6 2.4 custom-call.7
  192.1 1.1 fusion.10
  193.2 8.6 %fusion = f32[32,2048]{1,0:T(8,128)} fusion(f32[32,1024]{1,0:T(8,128)S(1)} %fusion.10, bf16[1,1024,2048]{2,1,0:T(8,128)(2,1)} %param.5, bf16[1,1024,2048]{2,1,0:T(8,128)(2,1)} %param.4), kind=kOutput, calls=%fused_computation.1 | convolution fusion | flops 811597824 | bytes 8781824 | tf_op jit(solution)/shard_map/dot_general | solution.py:24
  201.7 0.0 all-reduce.5.cloned.1.call-update
  201.8 0.0 copy-done.2
  201.8 0.2 copy.8
  202.0 248.0 %all-reduce.5.cloned.1.call-done = f32[32,2048]{1,0:T(8,128)} async-done(((f32[32,2048]{1,0:T(8,128)}), f32[32,2048]{1,0:T(8,128)}) %all-reduce.5.cloned.1.call-update) | async-done | bytes 262160 | tf_op jit(solution)/shard_map/psum | solution.py:27
  450.0 0.0 copy-start
  450.0 10.0 %fusion.13 = f32[1024,2048]{1,0:T(8,128)} fusion(f32[32,1024]{1,0:T(8,128)S(1)} %fusion.10, f32[32,2048]{1,0:T(8,128)} %all-reduce.5.cloned.1.call-done), kind=kOutput, calls=%fused_computation.22 | convolution fusion | flops 805371904 | bytes 8781824 | tf_op jit(solution)/shard_map/dot_general | solution.py:31
  459.9 0.0 copy-done
  459.9 0.0 copy-start.1
  459.9 9.2 %fusion.5 = bf16[1,1024,2048]{2,1,0:T(8,128)(2,1)} fusion(f32[1024,2048]{1,0:T(8,128)} %fusion.13, bf16[1,1024,2048]{2,1,0:T(8,128)(2,1)S(1)} %copy-done, bf16[1,1024,2048]{2,1,0:T(8,128)(2,1)} %param.4), kind=kLoop, calls=%fused_computation.7 | loop fusion | flops 10485760 | bytes 20971520 | tf_op jit(solution)/shard_map/broadcast_in_dim | solution.py:32
  469.2 1.2 dynamic-slice_add_fusion
  470.4 0.9 copy.9
  471.3 0.0 copy-done.1
  471.3 0.6 constant_dynamic-slice_fusion
  (3 shorter events, 0.1 us)
Async XLA Ops:
  7.2 164.0 %all-reduce.3.cloned.1.call-start = ((), (), s32[]{:S(2)}) async-start(), calls=%async_computation | async-start | bytes 131072 | tf_op jit(solution)/shard_map/psum | solution.py:17
  20.7 181.1 %copy-start.2 = (f32[1024,64]{0,1:T(8,128)S(1)}, f32[1024,64]{0,1:T(8,128)}, u32[]{:S(2)}) copy-start(f32[1024,64]{0,1:T(8,128)} %param.7) | copy-start | bytes 786436
  29.8 420.2 %all-reduce.5.cloned.1.call-start = ((), (), s32[]{:S(2)}) async-start(), calls=%async_computation.1 | async-start | bytes 524288 | tf_op jit(solution)/shard_map/psum | solution.py:27
  450.0 10.0 %copy-start = (bf16[1,1024,2048]{2,1,0:T(8,128)(2,1)S(1)}, bf16[1,1024,2048]{2,1,0:T(8,128)(2,1)}, u32[]{:S(2)}) copy-start(bf16[1,1024,2048]{2,1,0:T(8,128)(2,1)} %param.5) | copy-start | bytes 12582916
  459.9 11.4 %copy-start.1 = (f32[32,2048]{1,0:T(8,128)S(1)}, f32[32,2048]{1,0:T(8,128)}, u32[]{:S(2)}) copy-start(f32[32,2048]{1,0:T(8,128)} %all-reduce.5.cloned.1.call-done) | copy-start | bytes 786436
Sparse Core Ops, SparseCore 0:
  29.9 141.2 all-reduce.2
  201.9 248.0 all-reduce.4
where the time goes:
time: 479 us
  waiting for transfers between devices  389 us (81%)
  matrix products  29 us (6%)
  blocking collectives  27.3 us (6%)
  other arithmetic  17.2 us (4%)
  between operations  14.1 us (3%)
    psum x1, waiting for transfers between devices, shards(): right_full = lax.psum(right_term, ('replica', 'shard')) / replicas  248 us
    psum x1, waiting for transfers between devices, shards(): lax.psum(product.astype(jnp.bfloat16), 'replica').astype(jnp.float32)  141 us
    all_gather x1, blocking collectives, shards(): lax.all_gather(factor.astype(jnp.bfloat16), 'shard', axis=0, tiled=True)  13.8 us
    all_gather x1, blocking collectives, shards(): lax.all_gather(q_prev, 'shard', axis=1, tiled=True).astype(jnp.float32)  13.5 us
    dot_general x1, matrix products, shards(): approx = jnp.dot(ortho, right_full, precision=highest)  9.98 us
  transfers between devices with their start and end apart: 2, of which 2 were waited for; matrix products, arithmetic and copies ran while one was open for 0% of the time, Pallas kernels for 0%

commit v1 on v0

--- a/solution.py
+++ b/solution.py
@@ -24,7 +24,7 @@
     right_term = jnp.dot(ortho.T, merged, precision=highest)
     replicas = lax.axis_size("replica")
     block_width = col_count // lax.axis_size("shard")
-    right_full = lax.psum(right_term, ("replica", "shard")) / replicas
+    right_full = lax.psum(lax.psum(right_term, "replica"), "shard") / replicas
     q_next = lax.dynamic_slice_in_dim(
         right_full, lax.axis_index("shard") * block_width, block_width, 1
     )

time: 479 us -> 437 us (0.912)
  waiting for transfers between devices: 389 us -> 347 us
    psum x1 -> x2, waiting for transfers between devices: 248 us -> 206 us  [shards(): right_full = lax.psum(lax.psum(right_term, 'replica'), 'shard') / replicas]
  transfers between devices with their start and end apart: 2 -> 3, of which waited for: 2 -> 3; matrix products, arithmetic and copies ran while one was open for 0% -> 0% of each run, Pallas kernels for 0% -> 0%
where the time goes in v1:
time: 437 us; the launch traced here: 436 us
  waiting for transfers between devices  347 us (79%)
  matrix products  29 us (7%)
  blocking collectives  27.1 us (6%)
  other arithmetic  17.2 us (4%)
  between operations  13.8 us (3%)
    psum x2, waiting for transfers between devices, shards(): right_full = lax.psum(lax.psum(right_term, 'replica'), 'shard') / replicas  206 us
    psum x1, waiting for transfers between devices, shards(): lax.psum(product.astype(jnp.bfloat16), 'replica').astype(jnp.float32)  141 us
    all_gather x1, blocking collectives, shards(): lax.all_gather(factor.astype(jnp.bfloat16), 'shard', axis=0, tiled=True)  13.6 us
    all_gather x1, blocking collectives, shards(): lax.all_gather(q_prev, 'shard', axis=1, tiled=True).astype(jnp.float32)  13.5 us
    dot_general x1, matrix products, shards(): approx = jnp.dot(ortho, right_full, precision=highest)  9.98 us
    broadcast_in_dim x1, other arithmetic, shards(): new_errors = (merged - approx).astype(jnp.bfloat16)[None]  9.22 us
    dot_general x1, matrix products, shards(): lax.dot_general(merged, lax.all_gather(q_prev, 'shard', axis=1, tiled=Tru...  9.05 us
  transfers between devices with their start and end apart: 3, of which 3 were waited for; matrix products, arithmetic and copies ran while one was open for 0% of the time, Pallas kernels for 0%

profile of v1, /device:TPU:2, one launch (start us, length us, event | category | flops | bytes accessed | tf_op | source)
XLA Modules:
  0.0 436.4 jit_solution(10297928092489798604)
XLA Ops:
  7.2 0.0 all-reduce.4.cloned.1.call-start
  7.2 13.5 %all_gather.6 = bf16[32,2048]{1,0:T(8,128)(2,1)S(1)} all-gather(bf16[32,256]{1,0:T(8,128)(2,1)} %param.6), channel_id=1, replica_groups=mesh['replica'=32,'shard'=8] {'shard'}, dimensions={1}, use_global_device_ids=true | all-gather | bytes 147456 | tf_op jit(solution)/shard_map/all_gather | solution.py:13
  20.7 0.0 copy-start.2
  20.7 9.1 %fusion.6 = bf16[1024,32]{0,1:T(8,128)(2,1)} fusion(bf16[32,2048]{1,0:T(8,128)(2,1)S(1)} %all_gather.6, bf16[1,1024,2048]{2,1,0:T(8,128)(2,1)} %param.5, bf16[1,1024,2048]{2,1,0:T(8,128)(2,1)} %param.4), kind=kOutput, calls=%fused_computation.8 | convolution fusion | flops 811630592 | bytes 8585216 | tf_op jit(solution)/shard_map/dot_general | solution.py:11
  29.8 0.0 all-reduce.4.cloned.1.call-update
  29.8 0.0 all-reduce.6.cloned.1.call-start
  29.8 141.3 %all-reduce.4.cloned.1.call-done = bf16[1024,32]{0,1:T(8,128)(2,1)} async-done(((bf16[1024,32]{0,1:T(8,128)(2,1)}), bf16[1024,32]{0,1:T(8,128)(2,1)}) %all-reduce.4.cloned.1.call-update) | async-done | bytes 65552 | tf_op jit(solution)/shard_map/psum | solution.py:17
  171.2 13.6 %all_gather.7 = bf16[8192,32]{0,1:T(8,128)(2,1)S(1)} all-gather(bf16[1024,32]{0,1:T(8,128)(2,1)} %all-reduce.4.cloned.1.call-done), channel_id=1, replica_groups=mesh['replica'=32,'shard'=8] {'shard'}, dimensions={0}, use_global_device_ids=true | all-gather | bytes 589824 | tf_op jit(solution)/shard_map/all_gather | solution.py:18
  184.8 0.3 fusion.14
  185.1 0.1 copy.7
  185.2 2.9 cholesky.16
  188.1 0.6 compare_reduce_fusion
  188.8 0.7 fusion.9
  189.4 2.4 custom-call.7
  191.9 1.1 fusion.10
  193.0 8.6 %fusion = f32[32,2048]{1,0:T(8,128)} fusion(f32[32,1024]{1,0:T(8,128)S(1)} %fusion.10, bf16[1,1024,2048]{2,1,0:T(8,128)(2,1)} %param.5, bf16[1,1024,2048]{2,1,0:T(8,128)(2,1)} %param.4), kind=kOutput, calls=%fused_computation.1 | convolution fusion | flops 811597824 | bytes 8781824 | tf_op jit(solution)/shard_map/dot_general | solution.py:24
  201.6 0.0 all-reduce.6.cloned.1.call-update
  201.6 0.2 all-reduce.8.cloned.1.call-start
  201.8 140.6 %all-reduce.6.cloned.1.call-done = f32[32,2048]{1,0:T(8,128)} async-done(((f32[32,2048]{1,0:T(8,128)}), f32[32,2048]{1,0:T(8,128)}) %all-reduce.6.cloned.1.call-update) | async-done | bytes 262160 | tf_op jit(solution)/shard_map/psum | solution.py:27
  342.4 0.0 all-reduce.8.cloned.1.call-update
  342.4 0.0 copy-done.2
  342.4 0.2 copy.8
  342.6 65.2 %all-reduce.8.cloned.1.call-done = f32[32,2048]{1,0:T(8,128)} async-done(((f32[32,2048]{1,0:T(8,128)}), f32[32,2048]{1,0:T(8,128)}) %all-reduce.8.cloned.1.call-update) | async-done | bytes 262160 | tf_op jit(solution)/shard_map/psum | solution.py:27
  407.8 0.0 copy-start
  407.8 10.0 %fusion.13 = f32[1024,2048]{1,0:T(8,128)} fusion(f32[32,1024]{1,0:T(8,128)S(1)} %fusion.10, f32[32,2048]{1,0:T(8,128)} %all-reduce.8.cloned.1.call-done), kind=kOutput, calls=%fused_computation.22 | convolution fusion | flops 805371904 | bytes 8781824 | tf_op jit(solution)/shard_map/dot_general | solution.py:31
  417.8 0.0 copy-done
  417.8 0.0 copy-start.1
  417.8 9.2 %fusion.5 = bf16[1,1024,2048]{2,1,0:T(8,128)(2,1)} fusion(f32[1024,2048]{1,0:T(8,128)} %fusion.13, bf16[1,1024,2048]{2,1,0:T(8,128)(2,1)S(1)} %copy-done, bf16[1,1024,2048]{2,1,0:T(8,128)(2,1)} %param.4), kind=kLoop, calls=%fused_computation.7 | loop fusion | flops 10485760 | bytes 20971520 | tf_op jit(solution)/shard_map/broadcast_in_dim | solution.py:32
  427.1 1.2 dynamic-slice_add_fusion
  428.3 0.9 copy.9
  429.2 0.0 copy-done.1
  429.2 0.6 constant_dynamic-slice_fusion
  (3 shorter events, 0.1 us)
Async XLA Ops:
  7.2 164.0 %all-reduce.4.cloned.1.call-start = ((), (), s32[]{:S(2)}) async-start(), calls=%async_computation | async-start | bytes 131072 | tf_op jit(solution)/shard_map/psum | solution.py:17
  20.7 321.7 %copy-start.2 = (f32[1024,64]{0,1:T(8,128)S(1)}, f32[1024,64]{0,1:T(8,128)}, u32[]{:S(2)}) copy-start(f32[1024,64]{0,1:T(8,128)} %param.7) | copy-start | bytes 786436
  29.8 312.6 %all-reduce.6.cloned.1.call-start = ((), (), s32[]{:S(2)}) async-start(), calls=%async_computation.1 | async-start | bytes 524288 | tf_op jit(solution)/shard_map/psum | solution.py:27
  201.6 206.3 %all-reduce.8.cloned.1.call-start = ((), (), s32[]{:S(2)}) async-start(), calls=%async_computation.2 | async-start | bytes 524288 | tf_op jit(solution)/shard_map/psum | solution.py:27
  407.8 10.0 %copy-start = (bf16[1,1024,2048]{2,1,0:T(8,128)(2,1)S(1)}, bf16[1,1024,2048]{2,1,0:T(8,128)(2,1)}, u32[]{:S(2)}) copy-start(bf16[1,1024,2048]{2,1,0:T(8,128)(2,1)} %param.5) | copy-start | bytes 12582916
  417.8 11.4 %copy-start.1 = (f32[32,2048]{1,0:T(8,128)S(1)}, f32[32,2048]{1,0:T(8,128)}, u32[]{:S(2)}) copy-start(f32[32,2048]{1,0:T(8,128)} %all-reduce.8.cloned.1.call-done) | copy-start | bytes 786436
Sparse Core Ops, SparseCore 0:
  29.9 141.2 all-reduce.3
  201.7 140.6 all-reduce.5
  344.7 63.1 all-reduce.7
